TPU v7x, 256 devices: a whole 4x4x8 slice. The times are simulated.
256 devices in a mesh: freq: 4 (over x), row: 8 (over y, core), col: 8 (over z).
Axes of the slice: x: 4, y: 4, z: 8, core: 2. Of those that a mesh axis runs over, the one named last changes fastest.
Arguments:
- operator: bfloat16 [4, 2, 12000, 12000], P('freq', None, 'row', 'col'), may hold values from -0.0390625 to 0.0390625
- recorded: bfloat16 [4, 2, 12000, 128], P('freq', None, 'row'), may hold values from -61 to 61
Outputs:
- solution: float32 [4, 2, 12000, 128], P('freq', None, 'col')
- residual: float32 [4, 2, 12000, 128], P('freq', None, 'row')
All inputs are finite; a program needn't handle non-finite values.
Results may differ from a plain program's by a relative error of at most 0.0044.
Values sent between devices are 32-bit elements; how exact they have to be, the bound alone decides.
A program may use at most 128 MiB of HBM per device.

v0:
```python
import jax
import jax.numpy as jnp
from jax import lax
from jax.sharding import PartitionSpec as P

ITERS = 2
epsilon = 1e-06


def forward_part(operator, vector):
    blocks = jnp.einsum("krc,lcs->klrs", operator[0], vector[0], preferred_element_type=jnp.float32)
    return jnp.stack([blocks[0, 0] - blocks[1, 1], blocks[0, 1] + blocks[1, 0]])[None]


def adjoint_part(operator, vector):
    blocks = jnp.einsum("krc,lrs->klcs", operator[0], vector[0], preferred_element_type=jnp.float32)
    return jnp.stack([blocks[0, 0] + blocks[1, 1], blocks[0, 1] - blocks[1, 0]])[None]


def forward_reduce(partial_value, left_vec, alpha_now):
    imaged = lax.psum(partial_value, "col")
    update = imaged - alpha_now * left_vec
    squares = lax.psum(jnp.sum(update * update), ("freq", "row"))
    return (imaged, update, jnp.sqrt(squares + epsilon))


def adjoint_reduce(partial_value, right_vec, beta_now):
    summed = lax.psum(partial_value, "row")
    update = summed - beta_now * right_vec
    squares = lax.psum(jnp.sum(update * update), ("freq", "col"))
    return (update, jnp.sqrt(squares + epsilon))


def shards(operator, recorded):
    observed = recorded.astype(jnp.float32)
    col_rows = operator.shape[3]
    sources = recorded.shape[3]
    beta_now = jnp.sqrt(lax.psum(jnp.sum(observed * observed), ("freq", "row")) + epsilon)
    left_vec = observed / beta_now
    right_vec = jnp.zeros((1, 2, col_rows, sources), jnp.float32)
    back, alpha_now = adjoint_reduce(
        adjoint_part(operator, left_vec.astype(jnp.bfloat16)), right_vec, beta_now
    )
    right_vec = back / alpha_now
    search = right_vec
    phi_bar = beta_now
    rho_bar = alpha_now
    solution = jnp.zeros((1, 2, col_rows, sources), jnp.float32)
    fitted = jnp.zeros_like(observed)
    search_image = fitted
    w_ratio = jnp.float32(0.0)
    for turn_index in range(ITERS):
        imaged, update, beta_now = forward_reduce(
            forward_part(operator, right_vec.astype(jnp.bfloat16)), left_vec, alpha_now
        )
        left_vec = update / beta_now
        if turn_index == 0:
            search_image = imaged
        else:
            search_image = imaged - w_ratio * search_image
        rho_now = jnp.sqrt(rho_bar * rho_bar + beta_now * beta_now)
        cosine = rho_bar / rho_now
        sine_val = beta_now / rho_now
        phi_now = cosine * phi_bar
        phi_bar = sine_val * phi_bar
        solution = solution + phi_now / rho_now * search
        fitted = fitted + phi_now / rho_now * search_image
        if turn_index + 1 < ITERS:
            back, alpha_now = adjoint_reduce(
                adjoint_part(operator, left_vec.astype(jnp.bfloat16)), right_vec, beta_now
            )
            right_vec = back / alpha_now
            w_ratio = sine_val * alpha_now / rho_now
            rho_bar = -cosine * alpha_now
            search = right_vec - w_ratio * search
    return (solution, observed - fitted)


def solution(mesh):
    in_specs = (P("freq", None, "row", "col"), P("freq", None, "row", None))
    out_specs = (P("freq", None, "col", None), P("freq", None, "row", None))
    return jax.shard_map(shards, mesh=mesh, in_specs=in_specs, out_specs=out_specs, check_vma=False)
```

profile of v0, /device:TPU:1, one launch (start us, length us, event | category | flops | bytes accessed | tf_op | source)
XLA Modules:
  0.0 721.2 jit_solution(233663717337705087)
XLA Ops:
  7.2 0.0 all-reduce.5.cloned.1.call-start
  7.2 2.1 fusion.20
  9.3 65.9 %psum.63 = f32[]{:T(128)} all-reduce(f32[]{:T(128)} %fusion.20), channel_id=1, replica_groups=mesh['freq'=4,'row'=8,'col'=8] {'freq','row'}, use_global_device_ids=true, to_apply=%region_1.0 | all-reduce | flops 1 | bytes 8 | tf_op jit(solution)/shard_map/psum | solution.py:38
  75.9 0.0 copy-start.2
  75.9 23.8 %copy.5 = bf16[2,1500,1500]{1,2,0:T(8,128)(2,1)} copy(bf16[2,1500,1500]{2,0,1:T(2,128)(2,1)} %bitcast.70) | data formatting | bytes 18000000 | tf_op jit(solution)/shard_map/squeeze | solution.py:16
  99.7 0.0 copy-done.2
  99.7 6.3 fusion.17
  106.0 0.1 fusion.30
  106.1 0.1 fusion.32
  106.2 1.2 maximum_bitcast_fusion
  107.5 0.0 all-reduce.5.cloned.1.call-update
  107.5 0.0 all-reduce.7.cloned.1.call-start
  107.5 67.9 %all-reduce.5.cloned.1.call-done = f32[1,2,1500,128]{3,2,1,0:T(8,128)} async-done(((f32[1,2,1500,128]{3,2,1,0:T(8,128)}), f32[1,2,1500,128]{3,2,1,0:T(8,128)}) %all-reduce.5.cloned.1.call-update) | async-done | bytes 1536016 | tf_op jit(solution)/shard_map/psum | solution.py:28
  175.4 0.0 copy-start
  175.4 2.5 multiply_reduce_fusion.3
  177.9 61.5 %psum.65 = f32[]{:T(128)} all-reduce(f32[]{:T(128)} %multiply_reduce_fusion.3), channel_id=1, replica_groups=mesh['freq'=4,'row'=8,'col'=8] {'freq','col'}, use_global_device_ids=true, to_apply=%region_4.0 | all-reduce | flops 1 | bytes 8 | tf_op jit(solution)/shard_map/psum | solution.py:30
  240.1 0.0 copy-done
  240.1 6.3 fusion.8
  246.5 0.2 fusion.29
  246.6 1.2 maximum_bitcast_fusion.1
  247.9 0.0 all-reduce.7.cloned.1.call-update
  247.9 0.0 all-reduce.9.cloned.1.call-start
  247.9 82.4 %all-reduce.7.cloned.1.call-done = f32[1,2,1500,128]{3,2,1,0:T(8,128)} async-done(((f32[1,2,1500,128]{3,2,1,0:T(8,128)}), f32[1,2,1500,128]{3,2,1,0:T(8,128)}) %all-reduce.7.cloned.1.call-update) | async-done | bytes 1536016 | tf_op jit(solution)/shard_map/psum | solution.py:21
  330.4 0.0 copy-start.1
  330.4 2.7 multiply_reduce_fusion.2
  333.1 67.5 %psum.67 = f32[]{:T(128)} all-reduce(f32[]{:T(128)} %multiply_reduce_fusion.2), channel_id=1, replica_groups=mesh['freq'=4,'row'=8,'col'=8] {'freq','row'}, use_global_device_ids=true, to_apply=%region_7.0 | all-reduce | flops 1 | bytes 8 | tf_op jit(solution)/shard_map/psum | solution.py:23
  401.3 0.0 copy-done.1
  401.3 8.2 %fusion.14 = f32[2,2,1500,128]{3,2,1,0:T(8,128)S(1)} fusion(bf16[2,1500,1500,1]{2,0,1,3:T(2,128)(2,1)} %bitcast.72, f32[]{:T(128)S(6)} %sqrt.23, f32[1,2,1500,128]{3,2,1,0:T(8,128)S(1)} %copy-done.1, f32[]{:T(128)S(6)} %sqrt.22, f32[]{:T(128)S(6)} %sqrt.21, bf16[1,2,1500,128]{3,1,2,0:T(2,128)(2,1)} %param.3), kind=kOutput, calls=%fused_computation.10 | convolution fusion | flops 2306304000 | bytes 14376012 | tf_op jit(solution)/shard_map/krc,lrs->klcs/dot_general | solution.py:16
  409.5 0.2 fusion.27
  409.6 1.2 maximum_bitcast_fusion.2
  410.9 0.0 all-reduce.9.cloned.1.call-update
  410.9 0.0 all-reduce.11.cloned.1.call-start
  411.0 61.3 %all-reduce.9.cloned.1.call-done = f32[1,2,1500,128]{3,2,1,0:T(8,128)} async-done(((f32[1,2,1500,128]{3,2,1,0:T(8,128)}), f32[1,2,1500,128]{3,2,1,0:T(8,128)}) %all-reduce.9.cloned.1.call-update) | async-done | bytes 1536016 | tf_op jit(solution)/shard_map/psum | solution.py:28
  472.2 2.4 multiply_reduce_fusion.1
  474.6 61.5 %psum.69 = f32[]{:T(128)} all-reduce(f32[]{:T(128)} %multiply_reduce_fusion.1), channel_id=1, replica_groups=mesh['freq'=4,'row'=8,'col'=8] {'freq','col'}, use_global_device_ids=true, to_apply=%region_10.0 | all-reduce | flops 1 | bytes 8 | tf_op jit(solution)/shard_map/psum | solution.py:30
  536.8 6.9 fusion.11
  543.7 0.2 fusion.25
  543.9 1.2 maximum_bitcast_fusion.3
  545.1 0.0 all-reduce.11.cloned.1.call-update
  545.3 82.4 %all-reduce.11.cloned.1.call-done = f32[1,2,1500,128]{3,2,1,0:T(8,128)} async-done(((f32[1,2,1500,128]{3,2,1,0:T(8,128)}), f32[1,2,1500,128]{3,2,1,0:T(8,128)}) %all-reduce.11.cloned.1.call-update) | async-done | bytes 1536016 | tf_op jit(solution)/shard_map/psum | solution.py:21
  627.7 2.6 multiply_reduce_fusion
  630.4 67.6 %psum.71 = f32[]{:T(128)} all-reduce(f32[]{:T(128)} %multiply_reduce_fusion), channel_id=1, replica_groups=mesh['freq'=4,'row'=8,'col'=8] {'freq','row'}, use_global_device_ids=true, to_apply=%region_13.0 | all-reduce | flops 1 | bytes 8 | tf_op jit(solution)/shard_map/psum | solution.py:23
  698.8 3.0 convert_subtract_fusion
  701.8 6.4 copy.14
  708.2 6.4 copy.15
Async XLA Ops:
  7.2 168.3 %all-reduce.5.cloned.1.call-start = ((), (), s32[]{:S(2)}) async-start(), calls=%async_computation | async-start | bytes 3080192 | tf_op jit(solution)/shard_map/psum | solution.py:28
  75.9 23.8 %copy-start.2 = (bf16[1,2,1500,128]{3,1,2,0:T(2,128)(2,1)S(1)}, bf16[1,2,1500,128]{3,1,2,0:T(2,128)(2,1)}, u32[]{:S(2)}) copy-start(bf16[1,2,1500,128]{3,1,2,0:T(2,128)(2,1)} %param.3) | copy-start | bytes 2304004
  107.5 222.9 %all-reduce.7.cloned.1.call-start = ((), (), s32[]{:S(2)}) async-start(), calls=%async_computation.1 | async-start | bytes 3080192 | tf_op jit(solution)/shard_map/psum | solution.py:21
  175.4 64.7 %copy-start = (f32[1,2,1500,128]{3,2,1,0:T(8,128)S(1)}, f32[1,2,1500,128]{3,2,1,0:T(8,128)}, u32[]{:S(2)}) copy-start(f32[1,2,1500,128]{3,2,1,0:T(8,128)} %all-reduce.5.cloned.1.call-done) | copy-start | bytes 4608004
  247.9 224.4 %all-reduce.9.cloned.1.call-start = ((), (), s32[]{:S(2)}) async-start(), calls=%async_computation.2 | async-start | bytes 3080192 | tf_op jit(solution)/shard_map/psum | solution.py:28
  330.4 70.9 %copy-start.1 = (f32[1,2,1500,128]{3,2,1,0:T(8,128)S(1)}, f32[1,2,1500,128]{3,2,1,0:T(8,128)}, u32[]{:S(2)}) copy-start(f32[1,2,1500,128]{3,2,1,0:T(8,128)} %all-reduce.7.cloned.1.call-done) | copy-start | bytes 4608004
  410.9 216.8 %all-reduce.11.cloned.1.call-start = ((), (), s32[]{:S(2)}) async-start(), calls=%async_computation.3 | async-start | bytes 3080192 | tf_op jit(solution)/shard_map/psum | solution.py:21
Sparse Core Ops, SparseCore 0:
  107.6 67.7 all-reduce.4
  248.0 82.3 all-reduce.6
  411.0 61.1 all-reduce.8
  545.3 82.3 all-reduce.10
where the time goes:
time: 722 us; the launch traced here: 721 us
  blocking collectives  324 us (45%)
  waiting for transfers between devices  294 us (41%)
  local copies, waits for them, and re-layouts  36.7 us (5%)
  matrix products  27.7 us (4%)
  other arithmetic  20.9 us (3%)
  between operations  17.7 us (2%)
    psum x2, waiting for transfers between devices, forward_reduce(): imaged = lax.psum(partial_value, 'col')  165 us
    psum x2, blocking collectives, forward_reduce(): squares = lax.psum(jnp.sum(update * update), ('freq', 'row'))  135 us
    psum x2, waiting for transfers between devices, adjoint_reduce(): summed = lax.psum(partial_value, 'row')  129 us
    psum x2, blocking collectives, adjoint_reduce(): squares = lax.psum(jnp.sum(update * update), ('freq', 'col'))  123 us
    psum x1, blocking collectives, shards(): lax.psum(jnp.sum(observed * observed), ('freq', 'row')) + epsilon  65.9 us
    squeeze x1, local copies, waits for them, and re-layouts, adjoint_part(): operator[0]  23.8 us
    dot_general x2, matrix products, adjoint_part(): jnp.einsum('krc,lrs->klcs', operator[0], vector[0], preferred_element_typ...  14.5 us
  transfers between devices with their start and end apart: 4, of which 4 were waited for; matrix products, arithmetic and copies ran while one was open for 0% of the time, Pallas kernels for 0%

commit v1 on v0

--- a/solution.py
+++ b/solution.py
@@ -5,6 +5,18 @@
 
 ITERS = 2
 epsilon = 1e-06
+
+
+def keep_up_limits_here(unit):
+    current_block = unit
+    dev_count = lax.axis_size("col")
+    for hop_no in [
+        [(src_i, src_i ^ j0) for src_i in range(dev_count)]
+        for j0 in (1, 2, 4, 8, 16)
+        if j0 < dev_count
+    ]:
+        current_block = current_block + lax.ppermute(current_block, "col", hop_no)
+    return current_block
 
 
 def forward_part(operator, vector):
@@ -18,7 +30,7 @@
 
 
 def forward_reduce(partial_value, left_vec, alpha_now):
-    imaged = lax.psum(partial_value, "col")
+    imaged = keep_up_limits_here(partial_value)
     update = imaged - alpha_now * left_vec
     squares = lax.psum(jnp.sum(update * update), ("freq", "row"))
     return (imaged, update, jnp.sqrt(squares + epsilon))

time: 722 us -> 976 us (1.35)
  blocking collectives: 324 us -> 467 us
  waiting for transfers between devices: 294 us -> 362 us
  local copies, waits for them, and re-layouts: 36.7 us -> 71 us
    ppermute x0 -> x6, waiting for transfers between devices: none -> 233 us  [keep_up_limits_here(): current_block = current_block + lax.ppermute(current_block, 'col', hop_no)]
    psum x2 -> x0, waiting for transfers between devices: 165 us -> none  [forward_reduce(): imaged = lax.psum(partial_value, 'col')]
    psum x2, blocking collectives: 135 us -> 278 us  [forward_reduce(): squares = lax.psum(jnp.sum(update * update), ('freq', 'row'))]
    add x0 -> x4, local copies, waits for them, and re-layouts: none -> 23.2 us  [keep_up_limits_here(): current_block = current_block + lax.ppermute(current_block, 'col', hop_no)]
    broadcast_in_dim x0 -> x2, local copies, waits for them, and re-layouts: none -> 11.2 us  [forward_part(): jnp.stack([blocks[0, 0] - blocks[1, 1], blocks[0, 1] + blocks[1, 0]])[None]]
  transfers between devices with their start and end apart: 4 -> 8, of which waited for: 4 -> 8; matrix products, arithmetic and copies ran while one was open for 0% -> 0% of each run, Pallas kernels for 0% -> 0%
where the time goes in v1:
time: 976 us; the launch traced here: 968 us
  blocking collectives  467 us (48%)
  waiting for transfers between devices  362 us (37%)
  local copies, waits for them, and re-layouts  71 us (7%)
  matrix products  27.8 us (3%)
  other arithmetic  20.4 us (2%)
  between operations  18.5 us (2%)
    psum x2, blocking collectives, forward_reduce(): squares = lax.psum(jnp.sum(update * update), ('freq', 'row'))  278 us
    ppermute x6, waiting for transfers between devices, keep_up_limits_here(): current_block = current_block + lax.ppermute(current_block, 'col', hop_no)  233 us
    psum x2, waiting for transfers between devices, adjoint_reduce(): summed = lax.psum(partial_value, 'row')  129 us
    psum x2, blocking collectives, adjoint_reduce(): squares = lax.psum(jnp.sum(update * update), ('freq', 'col'))  123 us
    psum x1, blocking collectives, shards(): lax.psum(jnp.sum(observed * observed), ('freq', 'row')) + epsilon  65.9 us
    squeeze x1, local copies, waits for them, and re-layouts, adjoint_part(): operator[0]  23.8 us
    add x4, local copies, waits for them, and re-layouts, keep_up_limits_here(): current_block = current_block + lax.ppermute(current_block, 'col', hop_no)  23.2 us
  transfers between devices with their start and end apart: 8, of which 8 were waited for; matrix products, arithmetic and copies ran while one was open for 0% of the time, Pallas kernels for 0%

profile of v1, /device:TPU:1, one launch (start us, length us, event | category | flops | bytes accessed | tf_op | source)
XLA Modules:
  0.0 967.6 jit_solution(16520764156395710637)
XLA Ops:
  7.2 2.1 fusion.20
  9.3 65.9 %psum.49 = f32[]{:T(128)} all-reduce(f32[]{:T(128)} %fusion.20), channel_id=1, replica_groups=mesh['freq'=4,'row'=8,'col'=8] {'freq','row'}, use_global_device_ids=true, to_apply=%region_1.0 | all-reduce | flops 1 | bytes 8 | tf_op jit(solution)/shard_map/psum | solution.py:50
  75.9 23.8 %copy.17 = bf16[2,1500,1500]{1,2,0:T(8,128)(2,1)} copy(bf16[2,1500,1500]{2,0,1:T(2,128)(2,1)} %bitcast.78) | data formatting | bytes 18000000 | tf_op jit(solution)/shard_map/squeeze | solution.py:28
  99.7 6.3 fusion.17
  106.2 1.2 maximum_bitcast_fusion
  107.5 67.9 %all-reduce.3.cloned.1.call-done = f32[1,2,1500,128]{3,2,1,0:T(8,128)} async-done(((f32[1,2,1500,128]{3,2,1,0:T(8,128)}), f32[1,2,1500,128]{3,2,1,0:T(8,128)}) %all-reduce.3.cloned.1.call-update) | async-done | bytes 1536016 | tf_op jit(solution)/shard_map/psum | solution.py:40
  175.4 2.5 multiply_reduce_fusion.3
  177.9 61.5 %psum.51 = f32[]{:T(128)} all-reduce(f32[]{:T(128)} %multiply_reduce_fusion.3), channel_id=1, replica_groups=mesh['freq'=4,'row'=8,'col'=8] {'freq','col'}, use_global_device_ids=true, to_apply=%region_4.0 | all-reduce | flops 1 | bytes 8 | tf_op jit(solution)/shard_map/psum | solution.py:42
  240.1 6.3 fusion.8
  246.5 0.2 fusion.29
  246.6 0.1 maximum_bitcast_fusion.1
  246.7 5.6 copy.22
  252.3 0.6 collective-permute-start
  252.9 18.9 %collective-permute-done = f32[1,2,1500,128]{3,1,2,0:T(2,128)S(1)} collective-permute-done((f32[1,2,1500,128]{3,1,2,0:T(2,128)S(1)}, f32[1,2,1500,128]{3,1,2,0:T(2,128)S(1)}, u32[]{:S(2)}, u32[]{:S(2)}) %collective-permute-start) | collective-permute-done | bytes 1536032 | tf_op jit(solution)/shard_map/ppermute | solution.py:18
  271.8 0.2 copy_add_fusion.5
  272.0 5.6 copy.24
  277.6 0.1 collective-permute-start.1
  277.7 60.5 %collective-permute-done.1 = f32[1,2,1500,128]{3,1,2,0:T(2,128)S(1)} collective-permute-done((f32[1,2,1500,128]{3,1,2,0:T(2,128)S(1)}, f32[1,2,1500,128]{3,1,2,0:T(2,128)S(1)}, u32[]{:S(2)}, u32[]{:S(2)}) %collective-permute-start.1) | collective-permute-done | bytes 1536032 | tf_op jit(solution)/shard_map/ppermute | solution.py:18
  338.1 0.3 copy_add_fusion.4
  338.4 5.6 copy.26
  344.0 0.1 collective-permute-start.2
  344.1 37.7 %collective-permute-done.2 = f32[1,2,1500,128]{3,1,2,0:T(2,128)S(1)} collective-permute-done((f32[1,2,1500,128]{3,1,2,0:T(2,128)S(1)}, f32[1,2,1500,128]{3,1,2,0:T(2,128)S(1)}, u32[]{:S(2)}, u32[]{:S(2)}) %collective-permute-start.2) | collective-permute-done | bytes 1536032 | tf_op jit(solution)/shard_map/ppermute | solution.py:18
  381.9 2.2 multiply_reduce_fusion.2
  384.1 138.3 %psum.52 = f32[]{:T(128)} all-reduce(f32[]{:T(128)} %get-tuple-element.6), channel_id=1, replica_groups=mesh['freq'=4,'row'=8,'col'=8] {'freq','row'}, use_global_device_ids=true, to_apply=%region_6.0 | all-reduce | flops 1 | bytes 8 | tf_op jit(solution)/shard_map/psum | solution.py:35
  523.1 8.3 fusion.14
  531.4 0.2 fusion.27
  531.6 1.3 maximum_bitcast_fusion.2
  532.9 60.7 %all-reduce.5.cloned.1.call-done = f32[1,2,1500,128]{3,2,1,0:T(8,128)} async-done(((f32[1,2,1500,128]{3,2,1,0:T(8,128)}), f32[1,2,1500,128]{3,2,1,0:T(8,128)}) %all-reduce.5.cloned.1.call-update) | async-done | bytes 1536016 | tf_op jit(solution)/shard_map/psum | solution.py:40
  593.5 2.4 multiply_reduce_fusion.1
  595.9 61.5 %psum.54 = f32[]{:T(128)} all-reduce(f32[]{:T(128)} %multiply_reduce_fusion.1), channel_id=1, replica_groups=mesh['freq'=4,'row'=8,'col'=8] {'freq','col'}, use_global_device_ids=true, to_apply=%region_9.0 | all-reduce | flops 1 | bytes 8 | tf_op jit(solution)/shard_map/psum | solution.py:42
  658.1 6.9 fusion.11
  665.0 0.2 fusion.25
  665.2 0.1 maximum_bitcast_fusion.3
  665.3 5.6 copy.32
  670.9 0.3 collective-permute-start.3
  671.2 18.9 %collective-permute-done.3 = f32[1,2,1500,128]{3,1,2,0:T(2,128)S(1)} collective-permute-done((f32[1,2,1500,128]{3,1,2,0:T(2,128)S(1)}, f32[1,2,1500,128]{3,1,2,0:T(2,128)S(1)}, u32[]{:S(2)}, u32[]{:S(2)}) %collective-permute-start.3) | collective-permute-done | bytes 1536032 | tf_op jit(solution)/shard_map/ppermute | solution.py:18
  690.0 0.2 copy_add_fusion.2
  690.2 5.6 copy.34
  695.8 0.1 collective-permute-start.4
  695.9 60.5 %collective-permute-done.4 = f32[1,2,1500,128]{3,1,2,0:T(2,128)S(1)} collective-permute-done((f32[1,2,1500,128]{3,1,2,0:T(2,128)S(1)}, f32[1,2,1500,128]{3,1,2,0:T(2,128)S(1)}, u32[]{:S(2)}, u32[]{:S(2)}) %collective-permute-start.4) | collective-permute-done | bytes 1536032 | tf_op jit(solution)/shard_map/ppermute | solution.py:18
  756.4 0.3 copy_add_fusion.1
  756.7 6.4 copy.36
  763.3 36.9 %collective-permute-done.5 = f32[1,2,1500,128]{3,1,2,0:T(2,128)} collective-permute-done((f32[1,2,1500,128]{3,1,2,0:T(2,128)}, f32[1,2,1500,128]{3,1,2,0:T(2,128)}, u32[]{:S(2)}, u32[]{:S(2)}) %collective-permute-start.5) | collective-permute-done | bytes 1536032 | tf_op jit(solution)/shard_map/ppermute | solution.py:18
  800.2 2.9 multiply_reduce_fusion
  803.1 139.6 %psum.55 = f32[]{:T(128)} all-reduce(f32[]{:T(128)} %multiply_reduce_fusion), channel_id=1, replica_groups=mesh['freq'=4,'row'=8,'col'=8] {'freq','row'}, use_global_device_ids=true, to_apply=%region_11.0 | all-reduce | flops 1 | bytes 8 | tf_op jit(solution)/shard_map/psum | solution.py:35
  943.5 4.0 convert_subtract_fusion
  947.5 6.4 copy.38
  953.9 6.4 copy.39
  (15 shorter events, 0.3 us)
Async XLA Ops:
  7.2 168.2 %all-reduce.3.cloned.1.call-start = ((), (), s32[]{:S(2)}) async-start(), calls=%async_computation | async-start | bytes 3080192 | tf_op jit(solution)/shard_map/psum | solution.py:40
  75.9 23.8 %copy-start.1 = (bf16[1,2,1500,128]{3,1,2,0:T(2,128)(2,1)S(1)}, bf16[1,2,1500,128]{3,1,2,0:T(2,128)(2,1)}, u32[]{:S(2)}) copy-start(bf16[1,2,1500,128]{3,1,2,0:T(2,128)(2,1)} %param.3) | copy-start | bytes 2304004
  107.5 486.1 %all-reduce.5.cloned.1.call-start = ((), (), s32[]{:S(2)}) async-start(), calls=%async_computation.1 | async-start | bytes 3080192 | tf_op jit(solution)/shard_map/psum | solution.py:40
  175.4 64.7 %copy-start = (f32[1,2,1500,128]{3,2,1,0:T(8,128)S(1)}, f32[1,2,1500,128]{3,2,1,0:T(8,128)}, u32[]{:S(2)}) copy-start(f32[1,2,1500,128]{3,2,1,0:T(8,128)} %all-reduce.3.cloned.1.call-done) | copy-start | bytes 4608004
  252.3 19.5 %collective-permute-start = (f32[1,2,1500,128]{3,1,2,0:T(2,128)S(1)}, f32[1,2,1500,128]{3,1,2,0:T(2,128)S(1)}, u32[]{:S(2)}, u32[]{:S(2)}) collective-permute-start(f32[1,2,1500,128]{3,1,2,0:T(2,128)S(1)} %copy.22), channel_id=1, source_target_pairs={{0,1},{1,0},{2,3},{3,2},{4,5},{5,4},{6,7},{7,6},{8,9},{9,8},{10,11... | collective-permute-start | bytes 4608008 | tf_op jit(solution)/shard_map/ppermute | solution.py:18
  277.6 60.6 %collective-permute-start.1 = (f32[1,2,1500,128]{3,1,2,0:T(2,128)S(1)}, f32[1,2,1500,128]{3,1,2,0:T(2,128)S(1)}, u32[]{:S(2)}, u32[]{:S(2)}) collective-permute-start(f32[1,2,1500,128]{3,1,2,0:T(2,128)S(1)} %copy.24), channel_id=1, source_target_pairs={{0,2},{1,3},{2,0},{3,1},{4,6},{5,7},{6,4},{7,5},{8,10},{9,11},{10,... | collective-permute-start | bytes 4608008 | tf_op jit(solution)/shard_map/ppermute | solution.py:18
  338.4 43.4 %copy-start.2 = (bf16[1,2,1500,128]{3,1,2,0:T(2,128)(2,1)S(1)}, bf16[1,2,1500,128]{3,1,2,0:T(2,128)(2,1)}, u32[]{:S(2)}) copy-start(bf16[1,2,1500,128]{3,1,2,0:T(2,128)(2,1)} %param.3) | copy-start | bytes 2304004
  344.0 37.8 %collective-permute-start.2 = (f32[1,2,1500,128]{3,1,2,0:T(2,128)S(1)}, f32[1,2,1500,128]{3,1,2,0:T(2,128)S(1)}, u32[]{:S(2)}, u32[]{:S(2)}) collective-permute-start(f32[1,2,1500,128]{3,1,2,0:T(2,128)S(1)} %copy.26), channel_id=1, source_target_pairs={{0,4},{1,5},{2,6},{3,7},{4,0},{5,1},{6,2},{7,3},{8,12},{9,13},{10,... | collective-permute-start | bytes 4608008 | tf_op jit(solution)/shard_map/ppermute | solution.py:18
  381.9 2.2 copy-start.3
  670.9 19.2 %collective-permute-start.3 = (f32[1,2,1500,128]{3,1,2,0:T(2,128)S(1)}, f32[1,2,1500,128]{3,1,2,0:T(2,128)S(1)}, u32[]{:S(2)}, u32[]{:S(2)}) collective-permute-start(f32[1,2,1500,128]{3,1,2,0:T(2,128)S(1)} %copy.32), channel_id=1, source_target_pairs={{0,1},{1,0},{2,3},{3,2},{4,5},{5,4},{6,7},{7,6},{8,9},{9,8},{10,11... | collective-permute-start | bytes 4608008 | tf_op jit(solution)/shard_map/ppermute | solution.py:18
  695.8 60.6 %collective-permute-start.4 = (f32[1,2,1500,128]{3,1,2,0:T(2,128)S(1)}, f32[1,2,1500,128]{3,1,2,0:T(2,128)S(1)}, u32[]{:S(2)}, u32[]{:S(2)}) collective-permute-start(f32[1,2,1500,128]{3,1,2,0:T(2,128)S(1)} %copy.34), channel_id=1, source_target_pairs={{0,2},{1,3},{2,0},{3,1},{4,6},{5,7},{6,4},{7,5},{8,10},{9,11},{10,... | collective-permute-start | bytes 4608008 | tf_op jit(solution)/shard_map/ppermute | solution.py:18
  763.1 37.1 %collective-permute-start.5 = (f32[1,2,1500,128]{3,1,2,0:T(2,128)}, f32[1,2,1500,128]{3,1,2,0:T(2,128)}, u32[]{:S(2)}, u32[]{:S(2)}) collective-permute-start(f32[1,2,1500,128]{3,1,2,0:T(2,128)} %copy.36), channel_id=1, source_target_pairs={{0,4},{1,5},{2,6},{3,7},{4,0},{5,1},{6,2},{7,3},{8,12},{9,13},{10,... | collective-permute-start | bytes 4608008 | tf_op jit(solution)/shard_map/ppermute | solution.py:18
Sparse Core Ops, SparseCore 0:
  107.6 67.7 all-reduce.2
  533.0 60.5 all-reduce.4
